TPU v7x, 32 devices: a whole 2x2x4 slice. The times are simulated.
32 devices in a mesh: rows: 8 (over z, x), ch: 4 (over y, core).
Axes of the slice: x: 2, y: 2, z: 4, core: 2. Of those that a mesh axis runs over, the one named last changes fastest.
Arguments:
- latent: float32 [4, 16, 160, 512], P(None, 'rows', None, 'ch'), may hold values from -12 to 12
- first_weight: float32 [27, 512, 512], P(None, 'ch'), may hold values from -0.0546875 to 0.0546875
- norm_gain: float32 [512], P('ch'), may hold values from 0.5 to 1.5
- norm_shift: float32 [512], P('ch'), may hold values from -3 to 3
- second_weight: float32 [27, 512, 256], replicated, may hold values from -0.0546875 to 0.0546875
- out_bias: float32 [256], replicated, may hold values from -3 to 3
Outputs:
- decoded: float32 [4, 32, 320, 256], P(None, ('rows', 'ch'))
All inputs are finite; a program needn't handle non-finite values.
Results may differ from a plain program's by a relative error of at most 0.0001.
Values sent between devices are 32-bit elements; how exact they have to be, the bound alone decides.
A program may use at most 320 MiB of HBM per device.

v0:
```python
import functools

import jax
import jax.numpy as jnp
from jax import lax
from jax.experimental import pallas as pl
from jax.experimental.pallas import tpu as pltpu
from jax.sharding import PartitionSpec as P

GROUPS = 32
epsilon = 1e-06
VMEM_LIMIT = 58 * 1024 * 1024


def split(value):
    high = value.astype(jnp.bfloat16)
    low = (value - high.astype(jnp.float32)).astype(jnp.bfloat16)
    return high, low


def shifted(value):
    count = value.shape[0]
    place = lax.broadcasted_iota(jnp.int32, value.shape, 0)
    left = jnp.where(place == 0, 0.0, pltpu.roll(value, 1, 0))
    right = jnp.where(place == count - 1, 0.0, pltpu.roll(value, count - 1, 0))
    return left, value, right


def dot(a, b):
    return jnp.dot(a, b, preferred_element_type=jnp.float32)


def store_shifted(target_ref, frame, row, value):
    width = value.shape[-1]
    for k, piece in enumerate(shifted(value)):
        high, low = split(piece)
        for place in (0, 1, 2) if frame == 0 else (frame + 2,):
            target_ref[place, row, :, k * width:(k + 1) * width] = high
            target_ref[place, row, :, (3 + k) * width:(4 + k) * width] = low


def remote(src, dst, send, recv, rows, ch):
    return pltpu.make_async_remote_copy(
        src_ref=src, dst_ref=dst, send_sem=send, recv_sem=recv,
        device_id={"rows": rows, "ch": ch}, device_id_type=pl.DeviceIdType.MESH,
    )


def block_kernel(
    ring, count,
    x_ref, gain_ref, shift_ref, bias_ref, w1_hbm, w2_hbm,
    out_ref,
    stage_ref, high_ref, low_ref, halo_ref, xc1_ref, acc1_ref, part_ref, partin_ref,
    sum_ref, sumin_ref, raw_ref, stats_ref, vec_ref, gs_ref, w2_ref, xc2_ref, acc2_ref, mix_ref,
    w1_sem, w2_sem, halo_send, halo_recv, gs_send, gs_recv, part_send, part_recv,
    sum_send, sum_recv, stats_send, stats_recv, gather_send, gather_recv,
    row_send, row_recv, vec_send, vec_recv,
):
    frames, height, breadth, inner = x_ref.shape
    half_width = raw_ref.shape[-1]
    r = lax.axis_index("rows")
    c = lax.axis_index("ch")
    u = lax.rem(c, 2)
    v = lax.div(c, 2)
    pair = c + 1 - 2 * u
    across = c + 2 - 4 * v
    other = 1 - v
    peers = 2 * ring

    for t in range(3):
        pltpu.make_async_copy(w1_hbm.at[pl.ds(9 * t, 9)], stage_ref.at[pl.ds(9 * t, 9)], w1_sem.at[t]).start()

    def w2_copy(i):
        half = v if i < 3 else other
        start = pl.multiple_of(half * half_width, half_width)
        return pltpu.make_async_copy(
            w2_hbm.at[pl.ds(9 * (i % 3), 9), pl.ds(start, half_width)], w2_ref.at[i % 2], w2_sem.at[i % 2]
        )

    w2_copy(0).start()
    w2_copy(1).start()

    barrier = pltpu.get_barrier_semaphore()

    def greet(rows, ch):
        pl.semaphore_signal(
            barrier, inc=1, device_id={"rows": rows, "ch": ch}, device_id_type=pl.DeviceIdType.MESH
        )

    @pl.loop(0, ring)
    def _(i):
        greet(i, pair)

        @pl.when(i != r)
        def _():
            greet(i, c)

    greet(r, across)
    pl.semaphore_wait(barrier, peers)

    up, down = r > 0, r < ring - 1
    halo_down = remote(x_ref.at[:, pl.ds(height - 1, 1)], halo_ref.at[0], halo_send.at[0], halo_recv.at[0], r + 1, c)
    halo_up = remote(x_ref.at[:, pl.ds(0, 1)], halo_ref.at[1], halo_send.at[1], halo_recv.at[1], r - 1, c)
    pl.when(down)(halo_down.start)
    pl.when(up)(halo_up.start)

    gs_ref[u] = jnp.zeros(gs_ref.shape[1:], jnp.float32)
    gs_ref[u, 0:1, :] = gain_ref[...]
    gs_ref[u, 1:2, :] = shift_ref[...]
    gs_copy = remote(gs_ref.at[u], gs_ref.at[u], gs_send, gs_recv, r, pair)
    gs_copy.start()

    for frame in range(frames):
        for row in range(height):
            store_shifted(xc1_ref, frame, row + 1, x_ref[frame, row])

    for t in range(3):
        pltpu.make_async_copy(w1_hbm.at[pl.ds(9 * t, 9)], stage_ref.at[pl.ds(9 * t, 9)], w1_sem.at[t]).wait()

        @pl.loop(3 * t, 3 * t + 3)
        def _(g):
            high, low = split(stage_ref[pl.ds(3 * g, 3)].reshape(3 * inner, 2 * half_width))
            for n in range(2):
                high_ref[n, g] = high[:, n * half_width:(n + 1) * half_width]
                low_ref[n, g] = low[:, n * half_width:(n + 1) * half_width]

    def first_step(row, n, t, tap):
        slab = xc1_ref[pl.ds(t, frames), pl.ds(row + tap, 1)].reshape(frames * breadth, 6 * inner)
        high = high_ref[n, 3 * t + tap]
        low = low_ref[n, 3 * t + tap]
        both = jnp.concatenate([high, high], axis=0)
        acc1_ref[...] += dot(slab, both) + dot(slab[:, :3 * inner], low)

    def inner_taps(row, n):
        acc1_ref[...] = jnp.zeros_like(acc1_ref)

        @pl.loop(0, 6)
        def _(i):
            first_step(row, n, lax.div(i, 2), 1 - row + lax.rem(i, 2))

    def outer_taps(row, n):
        @pl.loop(0, 3)
        def _(i):
            first_step(row, n, i, 2 * row)

    inner_taps(1 - u, other)

    @pl.when(up)
    def _():
        halo_down.wait_recv()

    @pl.when(down)
    def _():
        halo_up.wait_recv()

    @pl.when(r == 0)
    def _():
        halo_ref[0] = jnp.zeros(halo_ref.shape[1:], jnp.float32)

    @pl.when(r == ring - 1)
    def _():
        halo_ref[1] = jnp.zeros(halo_ref.shape[1:], jnp.float32)

    for frame in range(frames):
        store_shifted(xc1_ref, frame, 0, halo_ref[0, frame, 0])
        store_shifted(xc1_ref, frame, height + 1, halo_ref[1, frame, 0])
    outer_taps(1 - u, other)
    part_copies = [
        remote(part_ref.at[i], partin_ref.at[i], part_send.at[i], part_recv.at[i], r, pair) for i in range(2)
    ]
    part_ref[0] = acc1_ref[...]
    part_copies[0].start()

    inner_taps(u, other)
    outer_taps(u, other)
    part_copies[0].wait_recv()
    sum_ref[...] = acc1_ref[...] + partin_ref[0]
    sum_copy = remote(sum_ref, sumin_ref, sum_send, sum_recv, r, across)
    sum_copy.start()

    inner_taps(1 - u, v)
    outer_taps(1 - u, v)
    part_ref[1] = acc1_ref[...]
    part_copies[1].start()

    inner_taps(u, v)
    outer_taps(u, v)
    part_copies[1].wait_recv()
    acc1_ref[...] += partin_ref[1]
    sum_copy.wait_recv()
    mine = acc1_ref[...] + sumin_ref[...]
    raw_ref[other, v] = mine

    user = r + jnp.where(c == 1, 1, 0) - jnp.where(c == 2, 1, 0)
    source = r - jnp.where(c == 0, 1, 0) + jnp.where(c == 3, 1, 0)
    used = jnp.logical_and(user >= 0, user < ring)
    fed = jnp.logical_and(source >= 0, source < ring)
    gather = remote(raw_ref.at[other, v], raw_ref.at[v, v], gather_send, gather_recv, r, across)
    gather.start()
    row_copies = [
        remote(raw_ref.at[other, h], raw_ref.at[v, h], row_send.at[i], row_recv.at[i], user, pair)
        for i, h in enumerate((v, other))
    ]
    pl.when(used)(row_copies[0].start)

    slot = 2 * r + u
    stats_ref[slot] = jnp.zeros(stats_ref.shape[1:], jnp.float32)
    stats_ref[slot, 0:1, :] = jnp.sum(mine, axis=0, keepdims=True)
    stats_ref[slot, 1:2, :] = jnp.sum(mine * mine, axis=0, keepdims=True)

    def stats_copy(i):
        return remote(
            stats_ref.at[slot], stats_ref.at[slot], stats_send.at[i], stats_recv.at[slot],
            lax.div(i, 2), 2 * v + lax.rem(i, 2),
        )

    def stats_arrival(i):
        return remote(
            stats_ref.at[i], stats_ref.at[i], stats_send.at[i], stats_recv.at[i],
            lax.div(i, 2), 2 * v + lax.rem(i, 2),
        )

    @pl.loop(0, peers)
    def _(i):
        @pl.when(i != slot)
        def _():
            stats_copy(i).start()

    @pl.loop(0, peers)
    def _(i):
        @pl.when(i != slot)
        def _():
            stats_arrival(i).wait_recv()

    sums = jnp.sum(stats_ref[:, 0:2, :], axis=0)
    group = 2 * half_width // GROUPS
    line = lax.div(lax.broadcasted_iota(jnp.int32, (half_width, half_width), 0), group)
    column = lax.div(lax.broadcasted_iota(jnp.int32, (half_width, half_width), 1), group)
    members = (line == column).astype(jnp.float32)
    eight = jnp.concatenate([sums, jnp.zeros((6, half_width), jnp.float32)], axis=0)
    totals = jnp.dot(eight, members, precision=lax.Precision.HIGHEST, preferred_element_type=jnp.float32)
    mean = totals[0:1] / count
    variance = totals[1:2] / count - mean * mean
    gs_copy.wait_recv()
    gain = jnp.concatenate([gs_ref[0, 0:1, :], gs_ref[1, 0:1, :]], axis=1)
    vec_ref[v] = jnp.zeros(vec_ref.shape[1:], jnp.float32)
    vec_ref[v, 0:1, :] = mean
    vec_ref[v, 1:2, :] = gain / jnp.sqrt(variance + epsilon)
    vec_ref[v, 2:3, :] = jnp.concatenate([gs_ref[0, 1:2, :], gs_ref[1, 1:2, :]], axis=1)
    vec_copy = remote(vec_ref.at[v], vec_ref.at[v], vec_send, vec_recv, r, across)
    vec_copy.start()

    acc2_ref[...] = jnp.zeros_like(acc2_ref)
    odd = u.astype(jnp.float32)

    @pl.when(jnp.logical_not(fed))
    def _():
        raw_ref[v] = jnp.zeros(raw_ref.shape[1:], jnp.float32)

    def normalise(half):
        mean, scale, shift = (vec_ref[half, i:i + 1, :] for i in range(3))
        for row in range(2):
            keep = jnp.where(jnp.logical_or(fed, row != v), 1.0, 0.0)
            for frame in range(frames):
                value = raw_ref[row, half, frame * breadth:(frame + 1) * breadth, :]
                value = (value - mean) * scale + shift
                value = value / (1.0 + jnp.exp(-value))
                store_shifted(xc2_ref, frame, row, value * keep)

    def second_step(i):
        w2_copy(i).wait()
        w_ref = w2_ref.at[i % 2]
        t = i % 3
        for row in range(2):
            taps = []
            for col in range(3):
                middle = w_ref[3 + col]
                if row == 0:
                    taps.append(w_ref[col] + odd * middle)
                else:
                    taps.append(w_ref[6 + col] + (1.0 - odd) * middle)
            slab = xc2_ref[t:t + frames, row].reshape(frames * breadth, 6 * half_width)
            for q in range(2):
                both = [taps[0], taps[1] + taps[2]] if q == 0 else [taps[0] + taps[1], taps[2]]
                high, low = split(jnp.concatenate(both, axis=0))
                x_high = slab[:, q * half_width:(q + 2) * half_width]
                x_low = slab[:, (3 + q) * half_width:(5 + q) * half_width]
                acc2_ref[q] += dot(x_high, high) + dot(x_low, high) + dot(x_high, low)
        if i + 2 < 6:
            w2_copy(i + 2).start()

    pl.when(fed)(row_copies[0].wait_recv)
    normalise(v)
    for i in range(3):
        second_step(i)

    gather.wait_recv()
    pl.when(used)(row_copies[1].start)
    vec_copy.wait_recv()
    pl.when(fed)(row_copies[1].wait_recv)
    normalise(other)
    for i in range(3, 6):
        second_step(i)

    lanes = out_ref.shape[3] // 128
    for frame in range(frames):
        for q in range(2):
            rows = acc2_ref[q, frame * breadth:(frame + 1) * breadth, :] + bias_ref[...]
            for lane in range(lanes):
                mix_ref[lane, pl.ds(q, breadth, stride=2), :] = rows[:, lane * 128:(lane + 1) * 128]
        for lane in range(lanes):
            out_ref[frame, 0, :, lane * 128:(lane + 1) * 128] = mix_ref[lane]

    pl.when(down)(halo_down.wait_send)
    pl.when(up)(halo_up.wait_send)
    gs_copy.wait_send()
    part_copies[0].wait_send()
    part_copies[1].wait_send()
    sum_copy.wait_send()
    gather.wait_send()
    vec_copy.wait_send()

    @pl.when(used)
    def _():
        row_copies[0].wait_send()
        row_copies[1].wait_send()

    @pl.loop(0, peers)
    def _(i):
        @pl.when(i != slot)
        def _():
            stats_copy(i).wait_send()


def shards(latent, first_weight, norm_gain, norm_shift, second_weight, out_bias):
    frames, height, breadth, inner = latent.shape
    channels = first_weight.shape[-1]
    outer = second_weight.shape[-1]
    ring = lax.axis_size("rows")
    half = channels // 2
    pixels = frames * breadth
    count = float(frames * height * ring * breadth * (channels // GROUPS))
    f32, b16 = jnp.float32, jnp.bfloat16
    dma = pltpu.SemaphoreType.DMA
    vmem = pl.BlockSpec(memory_space=pltpu.VMEM)
    hbm = pl.BlockSpec(memory_space=pl.ANY)
    return pl.pallas_call(
        functools.partial(block_kernel, ring, count),
        out_shape=jax.ShapeDtypeStruct((frames, 1, 2 * breadth, outer), f32),
        in_specs=[vmem, vmem, vmem, vmem, hbm, hbm],
        out_specs=vmem,
        scratch_shapes=[
            pltpu.VMEM(first_weight.shape, f32),
            pltpu.VMEM((2, 9, 3 * inner, half), b16),
            pltpu.VMEM((2, 9, 3 * inner, half), b16),
            pltpu.VMEM((2, frames, 1, breadth, inner), f32),
            pltpu.VMEM((frames + 2, height + 2, breadth, 6 * inner), b16),
            pltpu.VMEM((pixels, half), f32),
            pltpu.VMEM((2, pixels, half), f32),
            pltpu.VMEM((2, pixels, half), f32),
            pltpu.VMEM((pixels, half), f32),
            pltpu.VMEM((pixels, half), f32),
            pltpu.VMEM((2, 2, pixels, half), f32),
            pltpu.VMEM((2 * ring, 8, half), f32),
            pltpu.VMEM((2, 8, half), f32),
            pltpu.VMEM((2, 8, inner), f32),
            pltpu.VMEM((2, 9, half, outer), f32),
            pltpu.VMEM((frames + 2, 2, breadth, 6 * half), b16),
            pltpu.VMEM((2, pixels, outer), f32),
            pltpu.VMEM((outer // 128, 2 * breadth, 128), f32),
            dma((3,)), dma((2,)), dma((2,)), dma((2,)), dma, dma, dma((2,)), dma((2,)),
            dma, dma, dma((2 * ring,)), dma((2 * ring,)), dma, dma,
            dma((2,)), dma((2,)), dma, dma,
        ],
        compiler_params=pltpu.CompilerParams(
            collective_id=0, has_side_effects=True, vmem_limit_bytes=VMEM_LIMIT
        ),
    )(
        latent, norm_gain.reshape(1, inner), norm_shift.reshape(1, inner), out_bias.reshape(1, outer),
        first_weight, second_weight,
    )


def solution(mesh):
    return jax.shard_map(
        shards,
        mesh=mesh,
        in_specs=(P(None, "rows", None, "ch"), P(None, "ch", None), P("ch"), P("ch"), P(), P()),
        out_specs=P(None, ("rows", "ch"), None, None),
        check_vma=False,
    )
```

profile of v0, /device:TPU:5, one launch (start us, length us, event | category | flops | bytes accessed | tf_op | source)
XLA Modules:
  0.0 84.1 jit_solution(578738897171526186)
XLA Ops:
  0.0 81.6 %shard_map.64 = f32[4,1,320,256]{3,2,1,0:T(8,128)} custom-call(f32[4,2,160,128]{3,2,1,0:T(8,128)} %x_ref.1, f32[1,128]{1,0:T(1,128)} %bitcast.4, f32[1,128]{1,0:T(1,128)} %bitcast.5, f32[1,256]{1,0:T(1,128)} %bitcast.3, f32[27,128,512]{2,1,0:T(8,128)} %w1_hbm.1, f32[27,512,256]{2,1,0:T(8,128)} %w2_hbm.1), custom_call_target="tpu_custom_call" | custom-call | tf_op jit(solution)/shard_map/pallas_call | solution.py:347
  81.6 2.5 %copy.8 = f32[4,1,320,256]{3,2,1,0:T(8,128)} copy(f32[4,1,320,256]{3,2,1,0:T(8,128)} %shard_map.64) | data formatting | bytes 2621440
where the time goes:
time: 84.6 us; the launch traced here: 84.1 us
  Pallas kernels  81.6 us (96%)
  local copies, waits for them, and re-layouts  2.46 us (3%)
    pallas_call x1, Pallas kernels, shards(): pl.pallas_call(functools.partial(block_kernel, ring, count), out_shape=ja...  81.6 us
    unnamed x1, local copies, waits for them, and re-layouts  2.46 us

commit v1 on v0

--- a/solution.py
+++ b/solution.py
@@ -99,10 +99,21 @@
     pl.semaphore_wait(barrier, peers)
 
     up, down = r > 0, r < ring - 1
-    halo_down = remote(x_ref.at[:, pl.ds(height - 1, 1)], halo_ref.at[0], halo_send.at[0], halo_recv.at[0], r + 1, c)
-    halo_up = remote(x_ref.at[:, pl.ds(0, 1)], halo_ref.at[1], halo_send.at[1], halo_recv.at[1], r - 1, c)
-    pl.when(down)(halo_down.start)
-    pl.when(up)(halo_up.start)
+    parts = 2
+    some = frames // parts
+    span = some * breadth
+    halo_down, halo_up = [], []
+    for p in range(parts):
+        when = pl.ds(p * some, some)
+        halo_down.append(remote(
+            x_ref.at[when, pl.ds(height - 1, 1)], halo_ref.at[0, when], halo_send.at[p], halo_recv.at[p], r + 1, c
+        ))
+        halo_up.append(remote(
+            x_ref.at[when, pl.ds(0, 1)], halo_ref.at[1, when],
+            halo_send.at[parts + p], halo_recv.at[parts + p], r - 1, c,
+        ))
+        pl.when(down)(halo_down[p].start)
+        pl.when(up)(halo_up[p].start)
 
     gs_ref[u] = jnp.zeros(gs_ref.shape[1:], jnp.float32)
     gs_ref[u, 0:1, :] = gain_ref[...]
@@ -124,34 +135,28 @@
                 high_ref[n, g] = high[:, n * half_width:(n + 1) * half_width]
                 low_ref[n, g] = low[:, n * half_width:(n + 1) * half_width]
 
-    def first_step(row, n, t, tap):
-        slab = xc1_ref[pl.ds(t, frames), pl.ds(row + tap, 1)].reshape(frames * breadth, 6 * inner)
+    def first_step(acc, row, n, t, tap, begin, length):
+        slab = xc1_ref[pl.ds(t + begin, length), pl.ds(row + tap, 1)].reshape(length * breadth, 6 * inner)
         high = high_ref[n, 3 * t + tap]
         low = low_ref[n, 3 * t + tap]
         both = jnp.concatenate([high, high], axis=0)
-        acc1_ref[...] += dot(slab, both) + dot(slab[:, :3 * inner], low)
-
-    def inner_taps(row, n):
-        acc1_ref[...] = jnp.zeros_like(acc1_ref)
+        acc[pl.ds(begin * breadth, length * breadth), :] += dot(slab, both) + dot(slab[:, :3 * inner], low)
+
+    def inner_taps(acc, row, n):
+        acc[...] = jnp.zeros(acc.shape, jnp.float32)
 
         @pl.loop(0, 6)
         def _(i):
-            first_step(row, n, lax.div(i, 2), 1 - row + lax.rem(i, 2))
-
-    def outer_taps(row, n):
+            first_step(acc, row, n, lax.div(i, 2), 1 - row + lax.rem(i, 2), 0, frames)
+
+    def outer_taps(acc, row, n, begin=0, length=frames):
         @pl.loop(0, 3)
         def _(i):
-            first_step(row, n, i, 2 * row)
-
-    inner_taps(1 - u, other)
-
-    @pl.when(up)
-    def _():
-        halo_down.wait_recv()
-
-    @pl.when(down)
-    def _():
-        halo_up.wait_recv()
+            first_step(acc, row, n, i, 2 * row, begin, length)
+
+    sent = [part_ref.at[0], part_ref.at[1]]
+    inner_taps(sent[0], 1 - u, other)
+    inner_taps(acc1_ref, u, other)
 
     @pl.when(r == 0)
     def _():
@@ -161,49 +166,63 @@
     def _():
         halo_ref[1] = jnp.zeros(halo_ref.shape[1:], jnp.float32)
 
-    for frame in range(frames):
-        store_shifted(xc1_ref, frame, 0, halo_ref[0, frame, 0])
-        store_shifted(xc1_ref, frame, height + 1, halo_ref[1, frame, 0])
-    outer_taps(1 - u, other)
-    part_copies = [
-        remote(part_ref.at[i], partin_ref.at[i], part_send.at[i], part_recv.at[i], r, pair) for i in range(2)
-    ]
-    part_ref[0] = acc1_ref[...]
-    part_copies[0].start()
-
-    inner_taps(u, other)
-    outer_taps(u, other)
-    part_copies[0].wait_recv()
-    sum_ref[...] = acc1_ref[...] + partin_ref[0]
-    sum_copy = remote(sum_ref, sumin_ref, sum_send, sum_recv, r, across)
-    sum_copy.start()
-
-    inner_taps(1 - u, v)
-    outer_taps(1 - u, v)
-    part_ref[1] = acc1_ref[...]
-    part_copies[1].start()
-
-    inner_taps(u, v)
-    outer_taps(u, v)
-    part_copies[1].wait_recv()
-    acc1_ref[...] += partin_ref[1]
-    sum_copy.wait_recv()
-    mine = acc1_ref[...] + sumin_ref[...]
-    raw_ref[other, v] = mine
+    part_copies, sum_copies = [], []
+    for p in range(parts):
+        pl.when(up)(halo_down[p].wait_recv)
+        pl.when(down)(halo_up[p].wait_recv)
+        for frame in range(p * some, (p + 1) * some):
+            store_shifted(xc1_ref, frame, 0, halo_ref[0, frame, 0])
+            store_shifted(xc1_ref, frame, height + 1, halo_ref[1, frame, 0])
+        where = pl.ds(p * span, span)
+        outer_taps(sent[0], 1 - u, other, p * some, some)
+        part_copies.append(remote(
+            part_ref.at[0, where], partin_ref.at[0, where], part_send.at[p], part_recv.at[p], r, pair
+        ))
+        part_copies[p].start()
+        outer_taps(acc1_ref, u, other, p * some, some)
+        part_copies[p].wait_recv()
+        sum_ref[where, :] = acc1_ref[where, :] + partin_ref[0, where, :]
+        sum_copies.append(remote(
+            sum_ref.at[where], sumin_ref.at[where], sum_send.at[p], sum_recv.at[p], r, across
+        ))
+        sum_copies[p].start()
+
+    inner_taps(sent[1], 1 - u, v)
+    outer_taps(sent[1], 1 - u, v)
+    part_copies.append(remote(
+        part_ref.at[1], partin_ref.at[1], part_send.at[parts], part_recv.at[parts], r, pair
+    ))
+    part_copies[parts].start()
+    inner_taps(acc1_ref, u, v)
+    outer_taps(acc1_ref, u, v)
+    part_copies[parts].wait_recv()
 
     user = r + jnp.where(c == 1, 1, 0) - jnp.where(c == 2, 1, 0)
     source = r - jnp.where(c == 0, 1, 0) + jnp.where(c == 3, 1, 0)
     used = jnp.logical_and(user >= 0, user < ring)
     fed = jnp.logical_and(source >= 0, source < ring)
-    gather = remote(raw_ref.at[other, v], raw_ref.at[v, v], gather_send, gather_recv, r, across)
-    gather.start()
-    row_copies = [
-        remote(raw_ref.at[other, h], raw_ref.at[v, h], row_send.at[i], row_recv.at[i], user, pair)
-        for i, h in enumerate((v, other))
-    ]
-    pl.when(used)(row_copies[0].start)
+    gathers, row_copies = [], []
+    for p in range(parts):
+        where = pl.ds(p * span, span)
+        gathers.append(remote(
+            raw_ref.at[other, v, where], raw_ref.at[v, v, where], gather_send.at[p], gather_recv.at[p], r, across
+        ))
+    for i, h in enumerate((v, other)):
+        for p in range(parts):
+            where = pl.ds(p * span, span)
+            row_copies.append(remote(
+                raw_ref.at[other, h, where], raw_ref.at[v, h, where],
+                row_send.at[parts * i + p], row_recv.at[parts * i + p], user, pair,
+            ))
+    for p in range(parts):
+        where = pl.ds(p * span, span)
+        sum_copies[p].wait_recv()
+        raw_ref[other, v, where, :] = acc1_ref[where, :] + partin_ref[1, where, :] + sumin_ref[where, :]
+        gathers[p].start()
+        pl.when(used)(row_copies[p].start)
 
     slot = 2 * r + u
+    mine = raw_ref[other, v]
     stats_ref[slot] = jnp.zeros(stats_ref.shape[1:], jnp.float32)
     stats_ref[slot, 0:1, :] = jnp.sum(mine, axis=0, keepdims=True)
     stats_ref[slot, 1:2, :] = jnp.sum(mine * mine, axis=0, keepdims=True)
@@ -289,15 +308,17 @@
         if i + 2 < 6:
             w2_copy(i + 2).start()
 
-    pl.when(fed)(row_copies[0].wait_recv)
+    for p in range(parts):
+        pl.when(fed)(row_copies[p].wait_recv)
     normalise(v)
-    for i in range(3):
-        second_step(i)
-
-    gather.wait_recv()
-    pl.when(used)(row_copies[1].start)
+    second_step(0)
+    for p in range(parts):
+        gathers[p].wait_recv()
+        pl.when(used)(row_copies[parts + p].start)
+        second_step(1 + p)
     vec_copy.wait_recv()
-    pl.when(fed)(row_copies[1].wait_recv)
+    for p in range(parts):
+        pl.when(fed)(row_copies[parts + p].wait_recv)
     normalise(other)
     for i in range(3, 6):
         second_step(i)
@@ -311,19 +332,18 @@
         for lane in range(lanes):
             out_ref[frame, 0, :, lane * 128:(lane + 1) * 128] = mix_ref[lane]
 
-    pl.when(down)(halo_down.wait_send)
-    pl.when(up)(halo_up.wait_send)
+    for p in range(parts):
+        pl.when(down)(halo_down[p].wait_send)
+        pl.when(up)(halo_up[p].wait_send)
     gs_copy.wait_send()
-    part_copies[0].wait_send()
-    part_copies[1].wait_send()
-    sum_copy.wait_send()
-    gather.wait_send()
     vec_copy.wait_send()
+    for copy in part_copies + sum_copies + gathers:
+        copy.wait_send()
 
     @pl.when(used)
     def _():
-        row_copies[0].wait_send()
-        row_copies[1].wait_send()
+        for copy in row_copies:
+            copy.wait_send()
 
     @pl.loop(0, peers)
     def _(i):
@@ -368,9 +388,9 @@
             pltpu.VMEM((frames + 2, 2, breadth, 6 * half), b16),
             pltpu.VMEM((2, pixels, outer), f32),
             pltpu.VMEM((outer // 128, 2 * breadth, 128), f32),
-            dma((3,)), dma((2,)), dma((2,)), dma((2,)), dma, dma, dma((2,)), dma((2,)),
-            dma, dma, dma((2 * ring,)), dma((2 * ring,)), dma, dma,
-            dma((2,)), dma((2,)), dma, dma,
+            dma((3,)), dma((2,)), dma((4,)), dma((4,)), dma, dma, dma((3,)), dma((3,)),
+            dma((2,)), dma((2,)), dma((2 * ring,)), dma((2 * ring,)), dma((2,)), dma((2,)),
+            dma((4,)), dma((4,)), dma, dma,
         ],
         compiler_params=pltpu.CompilerParams(
             collective_id=0, has_side_effects=True, vmem_limit_bytes=VMEM_LIMIT

time: 84.6 us -> 72.2 us (0.85)
  Pallas kernels: 81.6 us -> 69.6 us
    pallas_call x1, Pallas kernels: 81.6 us -> 69.6 us  [shards(): pl.pallas_call(functools.partial(block_kernel, ring, count), out_shape=ja...]
where the time goes in v1:
time: 72.2 us; the launch traced here: 72 us
  Pallas kernels  69.6 us (96%)
  local copies, waits for them, and re-layouts  2.46 us (3%)
    pallas_call x1, Pallas kernels, shards(): pl.pallas_call(functools.partial(block_kernel, ring, count), out_shape=ja...  69.6 us
    unnamed x1, local copies, waits for them, and re-layouts  2.46 us

profile of v1, /device:TPU:5, one launch (start us, length us, event | category | flops | bytes accessed | tf_op | source)
XLA Modules:
  0.0 72.0 jit_solution(16221264061946673743)
XLA Ops:
  0.0 69.6 %shard_map.64 = f32[4,1,320,256]{3,2,1,0:T(8,128)} custom-call(f32[4,2,160,128]{3,2,1,0:T(8,128)} %x_ref.1, f32[1,128]{1,0:T(1,128)} %bitcast.4, f32[1,128]{1,0:T(1,128)} %bitcast.5, f32[1,256]{1,0:T(1,128)} %bitcast.3, f32[27,128,512]{2,1,0:T(8,128)} %w1_hbm.1, f32[27,512,256]{2,1,0:T(8,128)} %w2_hbm.1), custom_call_target="tpu_custom_call" | custom-call | tf_op jit(solution)/shard_map/pallas_call | solution.py:367
  69.6 2.5 %copy.8 = f32[4,1,320,256]{3,2,1,0:T(8,128)} copy(f32[4,1,320,256]{3,2,1,0:T(8,128)} %shard_map.64) | data formatting | bytes 2621440
